TPU v7x, 32 devices: a whole 2x2x4 slice. The times are simulated.
32 devices in a mesh: groups: 2 (over x), row: 4 (over y, core), dp: 4 (over z).
Axes of the slice: x: 2, y: 2, z: 4, core: 2. Of those that a mesh axis runs over, the one named last changes fastest.
Arguments:
- snapshots: bfloat16 [1024, 4096], P(('groups', 'dp'), 'row'), parts along dimension 0, may hold values from -6 to 6
- enc_weight: bfloat16 [32, 128, 256], P(('row', 'dp')), may hold values from -0.09375 to 0.09375
- hidden_weight: bfloat16 [8192, 256], P('dp'), may hold values from -0.375 to 0.375
- hidden_bias: bfloat16 [8192], P('dp'), may hold values from -3 to 3
- block_weight: bfloat16 [32, 8, 128, 128], P(('row', 'dp')), may hold values from -0.25 to 0.25
- block_ids: int32 [32, 8], P('row'), may hold values from 0 to 63, all different within a row
- block_counts: int32 [32], P('row'), may hold values from 1 to 8, as said below
Outputs:
- enc_grad: float32 [64, 128, 256], P(('groups', 'row', 'dp')), parts along dimension 0
- hidden_weight_grad: float32 [16384, 256], P(('groups', 'dp')), parts along dimension 0
- hidden_bias_grad: float32 [16384], P(('groups', 'dp')), parts along dimension 0
- block_grad: float32 [64, 8, 128, 128], P(('groups', 'row', 'dp')), parts along dimension 0
There are 2 independent parts, one for each index of `groups`. A program takes and returns all parts, laid end to end along the dimension named above; an argument that names none is the same for every part. Nothing has to cross between parts.
Inputs may be any that keep to these rules, and one draw needn't show every extreme that they name: `block_ids`: the 8 block numbers of one tile are distinct. `block_counts`: the live slots of a tile are its first ones; some tile has all 8 live.
All inputs are finite; a program needn't handle non-finite values.
Results may differ from a plain program's by a relative error of at most 0.0043.
Values may be sent and summed in bfloat16 or wider, within the bound.
A program may use at most 128 MiB of HBM per device.

v0:
```python
import math

import jax
import jax.numpy as jnp
from jax import lax
from jax.sharding import PartitionSpec as P


def silu_slope(pre):
    sigma = jax.nn.sigmoid(pre)
    return sigma * (1.0 + pre * (1.0 - sigma))


def on_device(
    snapshots, enc_weight, hidden_weight, hidden_bias, block_weight, block_ids, block_counts
):
    batch, width_rows = snapshots.shape
    enc_all, block_all = (
        lax.all_gather(enc_weight, "dp", axis=0, tiled=True),
        lax.all_gather(block_weight, "dp", axis=0, tiled=True),
    )
    tiles = block_all.shape[0]
    blocks = block_all.shape[1]
    blk_size = block_all.shape[2]
    latent_dim = enc_all.shape[2]
    partial_latent = jnp.dot(
        snapshots, enc_all.reshape(width_rows, latent_dim), preferred_element_type=jnp.float32
    )
    latent = lax.psum(partial_latent, "row")
    latent_b = latent.astype(jnp.bfloat16)
    weight_all, bias_all = (
        lax.all_gather(hidden_weight, "dp", axis=0, tiled=True),
        lax.all_gather(hidden_bias, "dp", axis=0, tiled=True),
    )
    hidden_units = weight_all.shape[0]
    nblocks = hidden_units // blk_size
    pre = lax.dot_general(
        latent_b, weight_all, (((1,), (1,)), ((), ())), preferred_element_type=jnp.float32
    ) + bias_all.astype(jnp.float32)
    hidden = jax.nn.silu(pre).astype(jnp.bfloat16)
    live_slots = jnp.arange(blocks)[None, :] < block_counts[:, None]
    live_float = live_slots.astype(jnp.float32)
    tile_hidden = (
        jnp.take(hidden.reshape(batch, nblocks, blk_size), block_ids, axis=1)
        * live_slots.astype(jnp.bfloat16)[None, :, :, None]
    )
    output = jnp.einsum(
        "btkc,tkcd->btd", tile_hidden, block_all, preferred_element_type=jnp.float32
    )
    scale = 1.0 / math.sqrt(batch * lax.axis_size("dp"))
    snap_tiles = snapshots.reshape(batch, tiles, blk_size).astype(jnp.float32)
    misfit = ((output - snap_tiles) * scale).astype(jnp.bfloat16)
    back = (
        jnp.einsum("btd,tkcd->btkc", misfit, block_all, preferred_element_type=jnp.float32)
        * live_float[None, :, :, None]
    )
    onehot = (block_ids[:, :, None] == jnp.arange(nblocks)[None, None, :]).astype(jnp.float32)
    partial_adjoint = jnp.einsum(
        "btkc,tkn->bnc", back, onehot, precision=lax.Precision.HIGHEST
    ).reshape(batch, hidden_units)
    adjoint = lax.psum(partial_adjoint, "row")
    pre_grad = (adjoint * silu_slope(pre)).astype(jnp.bfloat16)
    bias_part = jnp.sum(pre_grad, axis=0, dtype=jnp.float32)
    weight_part = lax.dot_general(
        pre_grad, latent_b, (((0,), (0,)), ((), ())), preferred_element_type=jnp.float32
    )
    latent_grad = jnp.dot(pre_grad, weight_all, preferred_element_type=jnp.float32).astype(
        jnp.bfloat16
    )
    enc_part = lax.dot_general(
        snapshots, latent_grad, (((0,), (0,)), ((), ())), preferred_element_type=jnp.float32
    ).reshape(tiles, blk_size, latent_dim)
    block_part = jnp.einsum(
        "btkc,btd->tkcd", tile_hidden, misfit, preferred_element_type=jnp.float32
    )
    enc_grad, block_grad, weight_grad, bias_grad = (
        lax.psum_scatter(enc_part, "dp", scatter_dimension=0, tiled=True),
        lax.psum_scatter(block_part, "dp", scatter_dimension=0, tiled=True),
        lax.psum_scatter(weight_part, "dp", scatter_dimension=0, tiled=True),
        lax.psum_scatter(bias_part, "dp", scatter_dimension=0, tiled=True),
    )
    return (enc_grad, weight_grad, bias_grad, block_grad)


def solution(mesh):
    in_specs = (
        P(("groups", "dp"), "row"),
        P(("row", "dp"), None, None),
        P("dp", None),
        P("dp"),
        P(("row", "dp"), None, None, None),
        P("row", None),
        P("row"),
    )
    out_specs = (
        P(("groups", "row", "dp"), None, None),
        P(("groups", "dp"), None),
        P(("groups", "dp")),
        P(("groups", "row", "dp"), None, None, None),
    )
    return jax.shard_map(
        on_device, mesh=mesh, in_specs=in_specs, out_specs=out_specs, check_vma=False
    )
```

profile of v0, /device:TPU:11, one launch (start us, length us, event | category | flops | bytes accessed | tf_op | source)
XLA Modules:
  0.0 509.1 jit_solution(17323204640776790621)
XLA Ops:
  7.2 0.0 copy-start.5
  7.2 0.0 copy-start.6
  7.2 0.0 all-gather.3.cloned.1.call-start
  7.2 0.7 all-gather.3.cloned.1.call-update
  7.9 0.0 all-gather.5.cloned.1.call-start
  8.0 0.7 all-gather.5.cloned.1.call-update
  8.7 0.0 all-reduce.4.cloned.1.call-start
  8.7 1.1 copy.28
  9.8 15.1 %all_gather.12 = bf16[8,128,256]{2,1,0:T(8,128)(2,1)S(1)} all-gather(bf16[2,128,256]{2,1,0:T(8,128)(2,1)} %param.8), channel_id=1, replica_groups=mesh['groups'=2,'row'=4,'dp'=4] {'dp'}, dimensions={0}, use_global_device_ids=true | all-gather | bytes 655360 | tf_op jit(solution)/shard_map/all_gather | solution.py:19
  24.9 1.2 fusion.36
  26.1 14.7 %all_gather.14 = bf16[8192]{0:T(1024)(128)(2,1)S(1)} all-gather(bf16[2048]{0:T(1024)(128)(2,1)} %param.10), channel_id=1, replica_groups=mesh['groups'=2,'row'=4,'dp'=4] {'dp'}, dimensions={0}, use_global_device_ids=true | all-gather | bytes 20480 | tf_op jit(solution)/shard_map/all_gather | solution.py:33
  40.8 0.8 copy.24
  41.6 0.7 compare_select_fusion
  42.3 0.1 reshape.77
  42.3 0.1 copy.29
  42.5 17.0 %all-reduce.5 = bf16[128,256]{1,0:T(8,128)(2,1)S(1)} all-reduce(f32[128,256]{1,0:T(8,128)S(1)} %fusion.36), channel_id=1, replica_groups=mesh['groups'=2,'row'=4,'dp'=4] {'row'}, use_global_device_ids=true, to_apply=%region_0.0 | all-reduce | flops 32768 | bytes 196608 | tf_op jit(solution)/shard_map/psum | solution.py:29
  59.5 0.0 copy-done.5
  59.5 0.0 copy-done.6
  59.5 0.1 fusion.32
  59.6 32.7 %all-gather.3.cloned.1.call-done = bf16[8192,256]{1,0:T(8,128)(2,1)} async-done(((bf16[2048,256]{1,0:T(8,128)(2,1)}), bf16[8192,256]{1,0:T(8,128)(2,1)}) %all-gather.3.cloned.1.call-update) | async-done | bytes 4194320 | tf_op jit(solution)/shard_map/all_gather | solution.py:32
  92.4 3.7 convolution_add_fusion
  96.0 0.0 copy-start
  96.0 2.0 copy-done
  98.0 1.1 copy_bitcast_fusion.1
  99.1 2.1 gather_fusion
  101.2 3.3 copy.26
  104.5 0.0 copy-start.1
  104.6 33.9 %all-gather.5.cloned.1.call-done = bf16[8,8,128,128]{3,2,1,0:T(8,128)(2,1)} async-done(((bf16[2,8,128,128]{3,2,1,0:T(8,128)(2,1)}), bf16[8,8,128,128]{3,2,1,0:T(8,128)(2,1)}) %all-gather.5.cloned.1.call-update) | async-done | bytes 2097168 | tf_op jit(solution)/shard_map/all_gather | solution.py:20
  138.4 0.0 copy-start.3
  138.4 2.7 fusion.19
  141.2 0.0 copy-start.4
  141.2 0.7 copy-done.4
  141.9 0.0 copy-done.3
  141.9 0.7 multiply_bitcast_fusion
  142.6 0.0 copy-done.1
  142.6 4.8 fusion
  147.4 5.2 %copy.43 = f32[16,8,64,128]{3,1,2,0:T(8,128)} copy(f32[16,8,64,128]{3,2,1,0:T(8,128)S(1)} %bitcast.72) | data formatting | bytes 8388608
  152.6 0.0 all-reduce.4.cloned.1.call-update
  152.7 0.0 copy-start.2
  152.7 0.0 reduce-scatter.4.cloned.1.call-start
  152.7 86.0 %all-reduce.4.cloned.1.call-done = f32[128,8192]{1,0:T(8,128)} async-done(((f32[128,8192]{1,0:T(8,128)}), f32[128,8192]{1,0:T(8,128)}) %all-reduce.4.cloned.1.call-update) | async-done | bytes 4194320 | tf_op jit(solution)/shard_map/psum | solution.py:61
  238.7 4.3 convert_reduce_fusion
  243.1 0.0 copy-done.2
  243.1 3.5 convolution_bitcast_fusion
  246.5 1.4 copy.36
  247.9 0.0 reduce-scatter.4.cloned.1.call-update
  247.9 0.0 reduce-scatter.8.cloned.1.call-start
  248.0 4.3 fusion.2
  252.3 0.0 reduce-scatter.8.cloned.1.call-update
  252.3 0.0 reduce-scatter.6.cloned.1.call-start
  252.4 4.5 fusion.37
  256.9 0.0 copy-start.7
  256.9 0.0 reduce-scatter.6.cloned.1.call-update
  256.9 0.6 copy-done.7
  257.6 0.6 dynamic-slice
  258.8 14.5 %all-reduce = f32[8192]{0:T(1024)S(1)} all-reduce(f32[8192]{0:T(1024)S(1)} %get-tuple-element.4), channel_id=4, replica_groups=mesh['groups'=2,'row'=4,'dp'=4] {'dp'}, use_global_device_ids=true, to_apply=%region_5.6.clone | all-reduce | flops 8192 | bytes 65536
  273.3 0.6 dynamic-slice.1
  273.9 0.6 reduce-scatter.4.cloned.1.call-done
  274.4 80.2 %reduce-scatter.8.cloned.1.call-done = f32[2,8,128,128]{3,2,1,0:T(8,128)} async-done(((f32[8,8,128,128]{3,2,1,0:T(8,128)}), f32[2,8,128,128]{3,2,1,0:T(8,128)}) %reduce-scatter.8.cloned.1.call-update) | async-done | bytes 1048592 | tf_op jit(solution)/shard_map/reduce_scatter | solution.py:78
  354.7 147.6 %reduce-scatter.6.cloned.1.call-done = f32[2048,256]{1,0:T(8,128)} async-done(((f32[8192,256]{1,0:T(8,128)}), f32[2048,256]{1,0:T(8,128)}) %reduce-scatter.6.cloned.1.call-update) | async-done | bytes 2097168 | tf_op jit(solution)/shard_map/reduce_scatter | solution.py:79
  (2 shorter events, 0.0 us)
Async XLA Ops:
  7.2 52.4 %copy-start.5 = (s32[8,8]{1,0:T(8,128)S(1)}, s32[8,8]{1,0:T(8,128)}, u32[]{:S(2)}) copy-start(s32[8,8]{1,0:T(8,128)} %param.12) | copy-start | bytes 772
  7.2 52.4 %copy-start.6 = (s32[8]{0:T(128)S(1)}, s32[8]{0:T(128)}, u32[]{:S(2)}) copy-start(s32[8]{0:T(128)} %param.13) | copy-start | bytes 100
  7.2 85.2 %all-gather.3.cloned.1.call-start = ((), (), s32[]{:S(2)}) async-start(), calls=%async_computation.3 | async-start | bytes 5242880 | tf_op jit(solution)/shard_map/all_gather | solution.py:32
  7.9 130.5 %all-gather.5.cloned.1.call-start = ((), (), s32[]{:S(2)}) async-start(), calls=%async_computation.4 | async-start | bytes 2621440 | tf_op jit(solution)/shard_map/all_gather | solution.py:20
  8.7 230.1 %all-reduce.4.cloned.1.call-start = ((), (), s32[]{:S(2)}) async-start(), calls=%async_computation.5 | async-start | bytes 8388608 | tf_op jit(solution)/shard_map/psum | solution.py:61
  96.0 2.0 copy-start
  104.5 38.0 %copy-start.1 = (bf16[8,8,128,128]{2,3,1,0:T(8,128)(2,1)}, bf16[8,8,128,128]{2,3,1,0:T(8,128)(2,1)S(1)}, u32[]{:S(2)}) copy-start(bf16[8,8,128,128]{2,3,1,0:T(8,128)(2,1)S(1)} %copy.26) | copy-start | bytes 6291460
  138.4 3.5 copy-start.3
  141.2 0.7 copy-start.4
  152.7 90.4 %copy-start.2 = (bf16[128,1024]{1,0:T(8,128)(2,1)S(1)}, bf16[128,1024]{1,0:T(8,128)(2,1)}, u32[]{:S(2)}) copy-start(bf16[128,1024]{1,0:T(8,128)(2,1)} %param.7) | copy-start | bytes 786436
  152.7 121.8 %reduce-scatter.4.cloned.1.call-start = ((), (), s32[]{:S(2)}) async-start(), calls=%async_computation.6 | async-start | bytes 1310720 | tf_op jit(solution)/shard_map/reduce_scatter | solution.py:77
  247.9 106.7 %reduce-scatter.8.cloned.1.call-start = ((), (), s32[]{:S(2)}) async-start(), calls=%async_computation.8 | async-start | bytes 5242880 | tf_op jit(solution)/shard_map/reduce_scatter | solution.py:78
  252.3 249.9 %reduce-scatter.6.cloned.1.call-start = ((), (), s32[]{:S(2)}) async-start(), calls=%async_computation.7 | async-start | bytes 10485760 | tf_op jit(solution)/shard_map/reduce_scatter | solution.py:79
  256.9 0.7 copy-start.7
Sparse Core Ops, SparseCore 0:
  9.6 82.7 all-gather.2
  93.9 44.4 all-gather.4
  152.8 85.9 all-reduce.3
  248.1 26.3 reduce-scatter.3
  277.2 77.4 reduce-scatter.7
  357.6 144.6 reduce-scatter.5
where the time goes:
time: 511 us; the launch traced here: 509 us
  waiting for transfers between devices  382 us (75%)
  blocking collectives  61.3 us (12%)
  matrix products  25.4 us (5%)
  local copies, waits for them, and re-layouts  18.6 us (4%)
  between operations  14.9 us (3%)
  other arithmetic  6.17 us (1%)
    reduce_scatter x1, waiting for transfers between devices, on_device(): lax.psum_scatter(weight_part, 'dp', scatter_dimension=0, tiled=True)  148 us
    psum x1, waiting for transfers between devices, on_device(): adjoint = lax.psum(partial_adjoint, 'row')  86 us
    reduce_scatter x1, waiting for transfers between devices, on_device(): lax.psum_scatter(block_part, 'dp', scatter_dimension=0, tiled=True)  80.2 us
    all_gather x1, waiting for transfers between devices, on_device(): lax.all_gather(block_weight, 'dp', axis=0, tiled=True)  33.9 us
    all_gather x1, waiting for transfers between devices, on_device(): lax.all_gather(hidden_weight, 'dp', axis=0, tiled=True)  32.7 us
    psum x1, blocking collectives, on_device(): latent = lax.psum(partial_latent, 'row')  17 us
    all_gather x1, blocking collectives, on_device(): lax.all_gather(enc_weight, 'dp', axis=0, tiled=True)  15.1 us
    all_gather x1, blocking collectives, on_device(): lax.all_gather(hidden_bias, 'dp', axis=0, tiled=True)  14.7 us
  transfers between devices with their start and end apart: 6, of which 6 were waited for; matrix products, arithmetic and copies ran while one was open for 5% of the time, Pallas kernels for 0%

commit v1 on v0

v1 whole, which is shorter than its diff:
```python
import functools
import math

import jax
import jax.numpy as jnp
from jax import lax
from jax.experimental import pallas as pl
from jax.experimental.pallas import tpu as pltpu
from jax.sharding import PartitionSpec as P

MESH = pl.DeviceIdType.MESH
F32 = jnp.float32
BF16 = jnp.bfloat16
VMEM_LIMIT = 56 * 1024 * 1024


def dot(a, b, ca=1, cb=0):
    return lax.dot_general(a, b, (((ca,), (cb,)), ((), ())), preferred_element_type=F32)


def greet(sizes):
    barrier = pltpu.get_barrier_semaphore()
    total = 0
    for axis, n in sizes.items():
        me = lax.axis_index(axis)
        for i in range(1, n):
            pl.semaphore_signal(
                barrier, inc=1, device_id={axis: lax.rem(me + i, n)}, device_id_type=MESH
            )
        total += n - 1
    pl.semaphore_wait(barrier, total)


class Exchange:
    def __init__(self, axis, n, src_of, dst_of, send, recv):
        self.axis, self.n, self.src_of, self.dst_of = axis, n, src_of, dst_of
        self.send, self.recv = send, recv
        self.me = lax.axis_index(axis)

    def copy(self, peer, slot):
        return pltpu.make_async_remote_copy(
            src_ref=self.src_of(peer),
            dst_ref=self.dst_of(slot),
            send_sem=self.send.at[peer],
            recv_sem=self.recv.at[slot],
            device_id={self.axis: peer},
            device_id_type=MESH,
        )

    def start(self):
        for i in range(1, self.n):
            self.copy(lax.rem(self.me + i, self.n), self.me).start()

    def wait_recv(self):
        for i in range(1, self.n):
            peer = lax.rem(self.me + i, self.n)
            self.copy(peer, peer).wait_recv()

    def wait_send(self):
        for i in range(1, self.n):
            self.copy(lax.rem(self.me + i, self.n), self.me).wait_send()


def forward_kernel(
    row, dp, snap, enc, weight, bias, block,
    hid, pre, lat_all, block_all, wq, snap_all,
    enc_all, bias_all, lat_part, dsend, drecv, rsend, rrecv, lsem,
):
    r, d = lax.axis_index("row"), lax.axis_index("dp")
    cols = snap.shape[1] // dp
    greet({"row": row, "dp": dp})

    def over_dp(k, src_of, dst):
        return Exchange("dp", dp, src_of, lambda s: dst.at[s], dsend.at[k], drecv.at[k])

    def snap_cols(p):
        return snap.at[:, pl.ds(pl.multiple_of(p * cols, cols), cols)]

    x_enc = over_dp(0, lambda p: enc, enc_all)
    x_bias = over_dp(1, lambda p: bias.at[r], bias_all)
    x_w = over_dp(2, lambda p: weight.at[r], wq)
    x_block = over_dp(3, lambda p: block, block_all)
    x_snap = over_dp(4, snap_cols, snap_all)
    x_enc.start()
    x_bias.start()
    x_w.start()
    own_block = pltpu.make_async_copy(block, block_all.at[d], lsem.at[0])
    own_snap = pltpu.make_async_copy(snap_cols(d), snap_all.at[d], lsem.at[1])
    own_block.start()
    own_snap.start()
    enc_all[d] = enc[...]
    bias_all[d] = bias[r]
    wq[d] = weight[r]
    x_enc.wait_recv()
    x_block.start()
    x_snap.start()
    part = jnp.zeros((snap.shape[0], enc.shape[1]), F32)
    for s in range(dp):
        part += dot(snap[:, s * cols : (s + 1) * cols], enc_all[s])
    lat_part[r] = part
    x_lat = Exchange("row", row, lambda p: lat_part.at[r], lambda s: lat_part.at[s], rsend.at[0], rrecv.at[0])
    x_lat.start()
    x_lat.wait_recv()
    total = lat_part[0]
    for s in range(1, row):
        total += lat_part[s]
    latent_b = total.astype(BF16)
    lat_all[d] = latent_b
    x_latb = over_dp(5, lambda p: lat_all.at[d], lat_all)
    x_latb.start()
    x_bias.wait_recv()
    x_w.wait_recv()
    ones = jnp.ones((bias.shape[1], snap.shape[0]), BF16)
    for s in range(dp):
        v = dot(wq[s], latent_b, 1, 1) + dot(bias_all[s], ones, 0, 0)
        pre[s] = v
        hid[s, r] = jax.nn.silu(v).astype(BF16)
    x_hid = Exchange("row", row, lambda p: hid.at[:, r], lambda s: hid.at[:, s], rsend.at[1], rrecv.at[1])
    x_hid.start()
    own_block.wait()
    own_snap.wait()
    for x in (x_hid, x_latb, x_block, x_snap):
        x.wait_recv()
    for x in (x_enc, x_bias, x_w, x_block, x_snap, x_lat, x_latb, x_hid):
        x.wait_send()


def decode_kernel(scale, ids, counts, hid, block, snap, slots_ref, mis_ref, adj_ref, adj):
    tiles, slots, blk, _ = block.shape
    adj[...] = jnp.zeros_like(adj)

    def tile(t, _):
        count = counts[t]
        out = jnp.zeros((snap.shape[0], blk), F32)
        for k in range(slots):
            live = (k < count).astype(F32)
            h = (hid[ids[t, k]].astype(F32) * live).astype(BF16)
            slots_ref[t, k] = h
            out += dot(h, block[t, k], 0, 0)
        here = snap[:, pl.ds(pl.multiple_of(t * blk, blk), blk)].astype(F32)
        misfit = ((out - here) * scale).astype(BF16)
        mis_ref[t] = misfit
        for k in range(slots):
            live = (k < count).astype(F32)
            adj[ids[t, k]] += dot(block[t, k], misfit, 1, 1) * live
        return 0

    lax.fori_loop(0, tiles, tile, 0)
    adj_ref[...] = adj[...].astype(BF16)


def backward_kernel(
    row, dp, adj, slots, mis, pre, lat_all, wq, snap_all,
    wgrad, bgrad, enc_grad, block_grad,
    adj_all, slots_all, mis_all, pg, pg_all, lg_part, lg_all,
    dsend, drecv, rsend, rrecv,
):
    r, d = lax.axis_index("row"), lax.axis_index("dp")
    greet({"row": row, "dp": dp})

    def over_dp(k, src_of, dst):
        return Exchange("dp", dp, src_of, lambda s: dst.at[s], dsend.at[k], drecv.at[k])

    def over_row(k, src_of, dst):
        return Exchange("row", row, src_of, lambda s: dst.at[s], rsend.at[k], rrecv.at[k])

    x_adj = over_row(0, lambda p: adj.at[:, p], adj_all)
    x_adj.start()
    x_mis = over_dp(0, lambda p: mis.at[p], mis_all)
    x_slots = over_dp(1, lambda p: slots.at[p], slots_all)
    x_mis.start()
    x_slots.start()
    adj_all[r] = adj[:, r]
    mis_all[d] = mis[d]
    slots_all[d] = slots[d]
    x_adj.wait_recv()
    part = jnp.zeros((mis.shape[2], lat_all.shape[2]), F32)
    for s in range(dp):
        a = adj_all[0, s].astype(F32)
        for q in range(1, row):
            a += adj_all[q, s].astype(F32)
        v = pre[s]
        sigma = jax.nn.sigmoid(v)
        g = (a * (sigma * (1.0 + v * (1.0 - sigma)))).astype(BF16)
        pg[s] = g
        part += dot(g, wq[s], 0, 0)
    pg_all[d] = pg[d]
    lg_part[r] = part
    x_lg = over_row(1, lambda p: lg_part.at[r], lg_part)
    x_pg = over_dp(2, lambda p: pg.at[p], pg_all)
    x_lg.start()
    x_pg.start()
    x_lg.wait_recv()
    total = lg_part[0]
    for s in range(1, row):
        total += lg_part[s]
    lg_all[d] = total.astype(BF16)
    x_lgb = over_dp(3, lambda p: lg_all.at[d], lg_all)
    x_lgb.start()
    x_pg.wait_recv()
    w = jnp.zeros(wgrad.shape[1:], F32)
    b = jnp.zeros(bgrad.shape[1:], F32)
    ones = jnp.ones((bgrad.shape[1], mis.shape[2]), BF16)
    for s in range(dp):
        w += dot(pg_all[s], lat_all[s])
        b += dot(ones, pg_all[s], 1, 1)
    wgrad[r] = w
    bgrad[r] = b
    x_w = over_row(2, lambda p: wgrad.at[r], wgrad)
    x_b = over_row(3, lambda p: bgrad.at[r], bgrad)
    x_w.start()
    x_b.start()
    x_mis.wait_recv()
    x_slots.wait_recv()

    def slot(k, _):
        for t in range(block_grad.shape[0]):
            o = dot(slots_all[0, t, k], mis_all[0, t])
            for s in range(1, dp):
                o += dot(slots_all[s, t, k], mis_all[s, t])
            block_grad[t, k] = o
        return 0

    lax.fori_loop(0, block_grad.shape[1], slot, 0)
    x_lgb.wait_recv()
    e = dot(snap_all[0], lg_all[0], 0, 0)
    for s in range(1, dp):
        e += dot(snap_all[s], lg_all[s], 0, 0)
    enc_grad[...] = e
    x_w.wait_recv()
    x_b.wait_recv()
    for x in (x_adj, x_mis, x_slots, x_lg, x_pg, x_lgb, x_w, x_b):
        x.wait_send()


def on_device(
    row, dp, snapshots, enc_weight, hidden_weight, hidden_bias, block_weight, block_ids, block_counts
):
    batch = snapshots.shape[0]
    own, slots, blk = block_weight.shape[:3]
    latent = enc_weight.shape[2]
    shard = hidden_weight.shape[0]
    part = shard // row
    tiles = own * dp
    cols = own * blk
    vmem = pl.BlockSpec(memory_space=pltpu.VMEM)
    smem = pl.BlockSpec(memory_space=pltpu.SMEM)
    dma = pltpu.SemaphoreType.DMA
    sds = jax.ShapeDtypeStruct
    bias = jnp.pad(hidden_bias.reshape(row, 1, part), ((0, 0), (0, 15), (0, 0)))
    hid, pre, lat_all, block_all, wq, snap_all = pl.pallas_call(
        functools.partial(forward_kernel, row, dp),
        out_shape=(
            sds((dp, row, part, batch), BF16),
            sds((dp, part, batch), F32),
            sds((dp, batch, latent), BF16),
            sds((dp, own, slots, blk, blk), BF16),
            sds((dp, part, latent), BF16),
            sds((dp, batch, cols), BF16),
        ),
        in_specs=[vmem] * 5,
        out_specs=[vmem] * 6,
        scratch_shapes=[
            pltpu.VMEM((dp, cols, latent), BF16),
            pltpu.VMEM((dp, 16, part), BF16),
            pltpu.VMEM((row, batch, latent), F32),
            dma((6, dp)), dma((6, dp)), dma((2, row)), dma((2, row)), dma((2,)),
        ],
        compiler_params=pltpu.CompilerParams(
            collective_id=0, has_side_effects=True, vmem_limit_bytes=VMEM_LIMIT
        ),
        name="forward",
    )(
        snapshots,
        enc_weight.reshape(cols, latent),
        hidden_weight.reshape(row, part, latent),
        bias,
        block_weight,
    )
    nblocks = dp * shard // blk
    scale = 1.0 / math.sqrt(batch * dp)
    tile_slots, misfit, adj = pl.pallas_call(
        functools.partial(decode_kernel, scale),
        out_shape=(
            sds((tiles, slots, blk, batch), BF16),
            sds((tiles, batch, blk), BF16),
            sds((nblocks, blk, batch), BF16),
        ),
        in_specs=[smem, smem, vmem, vmem, vmem],
        out_specs=[vmem] * 3,
        scratch_shapes=[pltpu.VMEM((nblocks, blk, batch), F32)],
        compiler_params=pltpu.CompilerParams(vmem_limit_bytes=VMEM_LIMIT),
        name="decode",
    )(
        block_ids,
        block_counts,
        hid.reshape(nblocks, blk, batch),
        block_all.reshape(tiles, slots, blk, blk),
        snapshots,
    )
    weight_grad, bias_grad, enc_grad, block_grad = pl.pallas_call(
        functools.partial(backward_kernel, row, dp),
        out_shape=(
            sds((row, part, latent), F32),
            sds((row, 8, part), F32),
            sds((cols, latent), F32),
            sds((own, slots, blk, blk), F32),
        ),
        in_specs=[vmem] * 7,
        out_specs=[vmem] * 4,
        scratch_shapes=[
            pltpu.VMEM((row, dp, part, batch), BF16),
            pltpu.VMEM((dp, own, slots, blk, batch), BF16),
            pltpu.VMEM((dp, own, batch, blk), BF16),
            pltpu.VMEM((dp, part, batch), BF16),
            pltpu.VMEM((dp, part, batch), BF16),
            pltpu.VMEM((row, batch, latent), F32),
            pltpu.VMEM((dp, batch, latent), BF16),
            dma((4, dp)), dma((4, dp)), dma((4, row)), dma((4, row)),
        ],
        compiler_params=pltpu.CompilerParams(
            collective_id=1, has_side_effects=True, vmem_limit_bytes=VMEM_LIMIT
        ),
        name="backward",
    )(
        adj.reshape(dp, row, part, batch),
        tile_slots.reshape(dp, own, slots, blk, batch),
        misfit.reshape(dp, own, batch, blk),
        pre,
        lat_all,
        wq,
        snap_all,
    )
    return (
        enc_grad.reshape(own, blk, latent),
        weight_grad.reshape(shard, latent),
        bias_grad[:, 0, :].reshape(shard),
        block_grad,
    )


def solution(mesh):
    in_specs = (
        P(("groups", "dp"), "row"),
        P(("row", "dp"), None, None),
        P("dp", None),
        P("dp"),
        P(("row", "dp"), None, None, None),
        P("row", None),
        P("row"),
    )
    out_specs = (
        P(("groups", "row", "dp"), None, None),
        P(("groups", "dp"), None),
        P(("groups", "dp")),
        P(("groups", "row", "dp"), None, None, None),
    )
    return jax.shard_map(
        functools.partial(on_device, mesh.shape["row"], mesh.shape["dp"]),
        mesh=mesh, in_specs=in_specs, out_specs=out_specs, check_vma=False,
    )
```

time: 511 us -> 216 us (0.42)
  waiting for transfers between devices: 382 us -> 0 us
  Pallas kernels: 0 us -> 206 us
  blocking collectives: 61.3 us -> 0 us
  matrix products: 25.4 us -> 0 us
  between operations: 14.9 us -> 0.65 us
  local copies, waits for them, and re-layouts: 18.6 us -> 8.56 us
  other arithmetic: 6.17 us -> 0 us
    reduce_scatter x3 -> x0, waiting for transfers between devices: 228 us -> none  [the longest x1 148 us: on_device(): lax.psum_scatter(weight_part, 'dp', scatter_dimension=0, tiled=True)]
    pallas_call x0 -> x3, Pallas kernels: none -> 206 us  [the longest x1 100 us: on_device(): pl.pallas_call(functools.partial(forward_kernel, row, dp), out_shape=(sds...]
    psum x1 -> x0, waiting for transfers between devices: 86 us -> none  [on_device(): adjoint = lax.psum(partial_adjoint, 'row')]
    all_gather x2 -> x0, waiting for transfers between devices: 66.6 us -> none  [the longest x1 33.9 us: on_device(): lax.all_gather(block_weight, 'dp', axis=0, tiled=True)]
    all_gather x2 -> x0, blocking collectives: 29.8 us -> none  [the longest x1 15.1 us: on_device(): lax.all_gather(enc_weight, 'dp', axis=0, tiled=True)]
    dot_general x8 -> x0, matrix products: 25.4 us -> none  [the longest x1 4.83 us: on_device(): jnp.einsum('btkc,tkn->bnc', back, onehot, precision=lax.Precision.HIGHEST)]
    psum x1 -> x0, blocking collectives: 17 us -> none  [on_device(): latent = lax.psum(partial_latent, 'row')]
    unnamed x1 -> x0, blocking collectives: 14.5 us -> none
  transfers between devices with their start and end apart: 6 -> 0, of which waited for: 6 -> 0; matrix products, arithmetic and copies ran while one was open for 5% -> 0% of each run, Pallas kernels for 0% -> 0%
where the time goes in v1:
time: 216 us; the launch traced here: 215 us
  Pallas kernels  206 us (95%)
  local copies, waits for them, and re-layouts  8.56 us (4%)
    pallas_call x1, Pallas kernels, on_device(): pl.pallas_call(functools.partial(forward_kernel, row, dp), out_shape=(sds...  100 us
    pallas_call x1, Pallas kernels, on_device(): pl.pallas_call(functools.partial(backward_kernel, row, dp), out_shape=(sd...  96.3 us
    pallas_call x1, Pallas kernels, on_device(): pl.pallas_call(functools.partial(decode_kernel, scale), out_shape=(sds((t...  9.36 us
    unnamed x5, local copies, waits for them, and re-layouts  5.78 us

profile of v1, /device:TPU:11, one launch (start us, length us, event | category | flops | bytes accessed | tf_op | source)
XLA Modules:
  0.0 215.1 jit_solution(4205867579856352740)
XLA Ops:
  0.6 0.7 reshape.48
  1.3 0.6 pad.4.bias
  2.0 100.3 %forward.1 = (bf16[4,4,512,128]{3,2,1,0:T(8,128)(2,1)}, f32[4,512,128]{2,1,0:T(8,128)}, bf16[4,128,256]{2,1,0:T(8,128)(2,1)}, bf16[4,2,8,128,128]{4,3,2,1,0:T(8,...) custom-call(bf16[128,1024]{1,0:T(8,128)(2,1)} %snap.3, bf16[256,256]{1,0:T(8,128)(2,1)} %bitcast.18, ...), custom_call_target="tpu_custom_call" | custom-call | tf_op jit(solution)/shard_map/forward/pallas_call | solution.py:251
  102.2 9.4 %decode.1 = (bf16[8,8,128,128]{3,2,1,0:T(8,128)(2,1)}, bf16[8,128,128]{2,1,0:T(8,128)(2,1)}, bf16[64,128,128]{2,1,0:T(8,128)(2,1)}) custom-call(s32[8,8]{1,0:T(8,128)} %ids.1, s32[8]{0:T(128)} %counts.1, bf16[64,128,128]{2,1,0:T(8,128)(2,1)} %bitcast.13, bf16[8,8,128,128]{3,2,1,0:T(8,128)(2,1)} %bitcast.14, bf16[128,1024]{1,0:T(8,128)(2,1)} %snap.3), custom_call_target="tpu_custom_call" | custom-call | tf_op jit(solution)/shard_map/decode/pallas_call | solution.py:282
  111.6 96.3 %backward.1 = (f32[4,512,256]{2,1,0:T(8,128)}, f32[4,8,512]{2,1,0:T(8,128)}, f32[256,256]{1,0:T(8,128)}, f32[2,8,128,128]{3,2,1,0:T(8,128)}) custom-call(bf16[4,4,512,128]{3,2,1,0:T(8,128)(2,1)} %bitcast.11, bf16[4,2,8,128,128]{4,3,2,1,0:T(8,128)(2,1)} %bitcast.10, bf16[4,2,128,128]{3,2,1,0:T(8,128)(2,1)} %bitcast.16, f32[4,512,128]{2,1,0:T(8,128)} %get-tuple-element.22.pre, ...), custom_call_target="tpu_custom_call" | custom-call | tf_op jit(solution)/shard_map/backward/pallas_call | solution.py:301
  207.9 1.4 slice.3
  209.3 1.7 copy.15
  211.0 0.0 copy-start
  211.0 3.1 %copy.16 = f32[2048,256]{1,0:T(8,128)} copy(f32[2048,256]{1,0:T(8,128)} %bitcast.12) | data formatting | bytes 4194304
  214.1 0.0 copy-done
  214.1 1.0 copy.17
Async XLA Ops:
  211.0 3.1 %copy-start = (f32[2,8,128,128]{3,2,1,0:T(8,128)S(1)}, f32[2,8,128,128]{3,2,1,0:T(8,128)}, u32[]{:S(2)}) copy-start(f32[2,8,128,128]{3,2,1,0:T(8,128)} %get-tuple-element.37) | copy-start | bytes 3145732

commit v2 on v1

v2 whole, which is shorter than its diff:
```python
import functools
import math

import jax
import jax.numpy as jnp
from jax import lax
from jax.experimental import pallas as pl
from jax.experimental.pallas import tpu as pltpu
from jax.sharding import PartitionSpec as P

MESH = pl.DeviceIdType.MESH
F32 = jnp.float32
BF16 = jnp.bfloat16
VMEM_LIMIT = 56 * 1024 * 1024


def dot(a, b, ca=1, cb=0):
    return lax.dot_general(a, b, (((ca,), (cb,)), ((), ())), preferred_element_type=F32)


def greet(sizes):
    barrier = pltpu.get_barrier_semaphore()
    total = 0
    for axis, n in sizes.items():
        me = lax.axis_index(axis)
        for i in range(1, n):
            pl.semaphore_signal(
                barrier, inc=1, device_id={axis: lax.rem(me + i, n)}, device_id_type=MESH
            )
        total += n - 1
    pl.semaphore_wait(barrier, total)


class Exchange:
    def __init__(self, axis, n, src_of, dst_of, send, recv):
        self.axis, self.n, self.src_of, self.dst_of = axis, n, src_of, dst_of
        self.send, self.recv = send, recv
        self.me = lax.axis_index(axis)

    def copy(self, peer, slot):
        return pltpu.make_async_remote_copy(
            src_ref=self.src_of(peer),
            dst_ref=self.dst_of(slot),
            send_sem=self.send.at[peer],
            recv_sem=self.recv.at[slot],
            device_id={self.axis: peer},
            device_id_type=MESH,
        )

    def start(self):
        for i in range(1, self.n):
            self.copy(lax.rem(self.me + i, self.n), self.me).start()

    def wait_recv(self):
        for i in range(1, self.n):
            peer = lax.rem(self.me + i, self.n)
            self.copy(peer, peer).wait_recv()

    def wait_send(self):
        for i in range(1, self.n):
            self.copy(lax.rem(self.me + i, self.n), self.me).wait_send()


class Chain:
    def __init__(self, axis, n, dst_of, send, recv):
        self.axis, self.n, self.dst_of = axis, n, dst_of
        self.send, self.recv = send, recv
        self.me = lax.axis_index(axis)

    def copy(self, slot, way, sem):
        return pltpu.make_async_remote_copy(
            src_ref=self.dst_of(slot),
            dst_ref=self.dst_of(slot),
            send_sem=self.send.at[sem],
            recv_sem=self.recv.at[slot],
            device_id={self.axis: self.me + way},
            device_id_type=MESH,
        )

    def each(self, step, act):
        me, n = self.me, self.n
        for way in (1, -1):
            slot = me - way * step
            sem = slot if step or way == 1 else n
            there, held = me + way, slot
            ok = (there >= 0) & (there < n) & (held >= 0) & (held < n)

            @pl.when(ok)
            def _():
                act(self.copy(slot, way, sem))

    def arrived(self, step):
        for way in (1, -1):
            slot = self.me - way * step

            @pl.when((slot >= 0) & (slot < self.n))
            def _():
                self.copy(slot, -way, slot).wait_recv()

    def start(self):
        self.each(0, lambda c: c.start())

    def forward(self, step):
        self.arrived(step)
        self.each(step, lambda c: c.start())

    def wait_send(self):
        for step in range(self.n - 1):
            self.each(step, lambda c: c.wait_send())


class RowRelay:
    def __init__(self, row, dst_of, send, recv):
        self.row, self.dst_of, self.send, self.recv = row, dst_of, send, recv
        self.me = lax.axis_index("row")
        self.sib = self.me + 1 - 2 * lax.rem(self.me, 2)
        self.peers = [lax.rem(self.me + 2 * i, row) for i in range(1, row // 2)]

    def copy(self, slot, to, sem):
        return pltpu.make_async_remote_copy(
            src_ref=self.dst_of(slot),
            dst_ref=self.dst_of(slot),
            send_sem=self.send.at[sem],
            recv_sem=self.recv.at[slot],
            device_id={"row": to},
            device_id_type=MESH,
        )

    def start(self):
        for p in self.peers:
            self.copy(self.me, p, p).start()
        self.copy(self.me, self.sib, self.sib).start()

    def forward(self):
        for p in self.peers:
            self.copy(p, p, p).wait_recv()
            self.copy(p, self.sib, self.row + p).start()

    def wait_recv(self):
        for p in [self.me, *self.peers]:
            slot = p + 1 - 2 * lax.rem(p, 2)
            self.copy(slot, self.sib, slot).wait_recv()

    def wait_send(self):
        for p in self.peers:
            self.copy(self.me, p, p).wait_send()
            self.copy(p, self.sib, self.row + p).wait_send()
        self.copy(self.me, self.sib, self.sib).wait_send()


def forward_kernel(
    row, dp, snap, enc, weight, bias, block,
    hid, pre, lat_all, block_all, w_all, snap_all, bias_all,
    enc_all, lat_part, dsend, drecv, csend, crecv, rsend, rrecv, wsend, wrecv, lsem,
):
    r, d = lax.axis_index("row"), lax.axis_index("dp")
    cols = snap.shape[1] // dp
    batch = snap.shape[0]
    greet({"row": row, "dp": dp})

    def over_dp(k, src_of, dst):
        return Exchange("dp", dp, src_of, lambda s: dst.at[s], dsend.at[k], drecv.at[k])

    def snap_cols(p):
        return snap.at[:, pl.ds(pl.multiple_of(p * cols, cols), cols)]

    def w_slot(s):
        return RowRelay(row, lambda q: w_all.at[s, q], wsend.at[s], wrecv.at[s])

    def w_arrived(step):
        x_w.forward(step)
        for way in (1, -1):
            s = d - way * step

            @pl.when((s >= 0) & (s < dp))
            def _():
                w_slot(s).start()

    x_enc = Chain("dp", dp, lambda s: enc_all.at[s], csend.at[0], crecv.at[0])
    x_w = Chain("dp", dp, lambda s: w_all.at[s, r], csend.at[1], crecv.at[1])
    x_block = Chain("dp", dp, lambda s: block_all.at[s], csend.at[2], crecv.at[2])
    x_bias = over_dp(0, lambda p: bias, bias_all)
    x_snap = over_dp(1, snap_cols, snap_all)
    own_block = pltpu.make_async_copy(block, block_all.at[d], lsem.at[0])
    own_snap = pltpu.make_async_copy(snap_cols(d), snap_all.at[d], lsem.at[1])
    own_block.start()
    own_snap.start()
    enc_all[d] = enc[...]
    x_enc.start()
    w_all[d, r] = weight[r]
    x_w.start()
    w_slot(d).start()
    bias_all[d] = bias[...]
    x_bias.start()
    for step in range(1, dp - 1):
        x_enc.forward(step)
        w_arrived(step)
    own_block.wait()
    x_block.start()
    x_snap.start()
    x_enc.forward(dp - 1)
    part = jnp.zeros((batch, enc.shape[1]), F32)
    for s in range(dp):
        part += dot(snap[:, s * cols : (s + 1) * cols], enc_all[s])
    lat_part[r] = part
    x_lat = Exchange("row", row, lambda p: lat_part.at[r], lambda s: lat_part.at[s], rsend, rrecv)
    x_lat.start()
    w_arrived(dp - 1)
    x_lat.wait_recv()
    total = lat_part[0]
    for s in range(1, row):
        total += lat_part[s]
    latent_b = total.astype(BF16)
    lat_all[d] = latent_b
    x_latb = over_dp(2, lambda p: lat_all.at[d], lat_all)
    x_latb.start()
    if dp > 2:
        x_block.forward(1)
    x_bias.wait_recv()
    lines = lax.broadcasted_iota(jnp.int32, (bias.shape[0], batch), 0)

    def pre_of(s, q):
        pick = jnp.where(lines == q, 1.0, 0.0).astype(BF16)
        return dot(w_all[s, q], lat_all[d], 1, 1) + dot(bias_all[s], pick, 0, 0)

    for s in range(dp):
        pre[s] = pre_of(s, r)
    for s in range(dp):
        w_slot(s).forward()
    for step in range(2, dp - 1):
        x_block.forward(step)

    def hid_of(s, _):
        w_slot(s).wait_recv()
        for q in range(row):
            hid[s, q] = jax.nn.silu(pre_of(s, q)).astype(BF16)
        return 0

    lax.fori_loop(0, dp, hid_of, 0)
    own_snap.wait()
    x_block.arrived(dp - 1)
    for x in (x_latb, x_snap):
        x.wait_recv()
    for x in (x_enc, x_bias, x_w, x_block, x_snap, x_lat, x_latb):
        x.wait_send()
    for s in range(dp):
        w_slot(s).wait_send()


def decode_kernel(scale, ids, counts, hid, block, snap, mis_ref, adj_ref, adj):
    tiles, slots, blk, _ = block.shape
    adj[...] = jnp.zeros_like(adj)

    def tile(t, _):
        count = counts[t]
        out = jnp.zeros((snap.shape[0], blk), F32)
        for k in range(slots):
            live = (k < count).astype(F32)
            out += dot(hid[ids[t, k]], block[t, k], 0, 0) * live
        here = snap[:, pl.ds(pl.multiple_of(t * blk, blk), blk)].astype(F32)
        misfit = ((out - here) * scale).astype(BF16)
        mis_ref[t] = misfit
        for k in range(slots):
            live = (k < count).astype(F32)
            adj[ids[t, k]] += dot(block[t, k], misfit, 1, 1) * live
        return 0

    lax.fori_loop(0, tiles, tile, 0)
    adj_ref[...] = adj[...].astype(BF16)


def block_grad_kernel(ids, counts, w, bias, lat, mis, grad):
    own, slots, blk, _ = grad.shape
    dp = mis.shape[0]
    ones = jnp.ones((bias.shape[1], mis.shape[2]), BF16)

    def slot(k, _):
        for t in range(own):
            j = ids[t, k]
            live = (k < counts[t]).astype(F32)
            shift = dot(bias[j], ones, 0, 0)
            o = jnp.zeros((blk, blk), F32)
            for s in range(dp):
                h = jax.nn.silu(dot(w[j], lat[s], 1, 1) + shift).astype(BF16)
                o += dot(h, mis[s, t])
            grad[t, k] = o * live
        return 0

    lax.fori_loop(0, slots, slot, 0)


def backward_kernel(
    row, dp, adj, mis, pre, lat_all, w_all, snap_all,
    wgrad, bgrad, enc_grad, mis_all,
    adj_all, pg, pg_all, lg_part, lg_all,
    dsend, drecv, rsend, rrecv, wsend, wrecv,
):
    r, d = lax.axis_index("row"), lax.axis_index("dp")
    greet({"row": row, "dp": dp})

    def over_dp(k, src_of, dst):
        return Exchange("dp", dp, src_of, lambda s: dst.at[s], dsend.at[k], drecv.at[k])

    def over_row(k, src_of, dst):
        return Exchange("row", row, src_of, lambda s: dst.at[s], rsend.at[k], rrecv.at[k])

    x_adj = over_row(0, lambda p: adj.at[:, p], adj_all)
    x_adj.start()
    x_mis = over_dp(0, lambda p: mis.at[p], mis_all)
    x_mis.start()
    adj_all[r] = adj[:, r]
    mis_all[d] = mis[d]
    x_adj.wait_recv()
    part = jnp.zeros((mis.shape[2], lat_all.shape[2]), F32)
    for s in range(dp):
        a = adj_all[0, s].astype(F32)
        for q in range(1, row):
            a += adj_all[q, s].astype(F32)
        v = pre[s]
        sigma = jax.nn.sigmoid(v)
        g = (a * (sigma * (1.0 + v * (1.0 - sigma)))).astype(BF16)
        pg[s] = g
    x_pg = over_dp(1, lambda p: pg.at[p], pg_all)
    x_pg.start()
    for s in range(dp):
        part += dot(pg[s], w_all[s, r], 0, 0)
    pg_all[d] = pg[d]
    lg_part[r] = part
    x_lg = over_row(1, lambda p: lg_part.at[r], lg_part)
    x_lg.start()
    x_lg.wait_recv()
    total = lg_part[0]
    for s in range(1, row):
        total += lg_part[s]
    lg_all[d] = total.astype(BF16)
    x_lgb = over_dp(2, lambda p: lg_all.at[d], lg_all)
    x_lgb.start()
    x_pg.wait_recv()
    w = jnp.zeros(wgrad.shape[1:], F32)
    b = jnp.zeros(bgrad.shape[1:], F32)
    ones = jnp.ones((bgrad.shape[1], mis.shape[2]), BF16)
    for s in range(dp):
        w += dot(pg_all[s], lat_all[s])
    wgrad[r] = w
    x_w = RowRelay(row, lambda q: wgrad.at[q], wsend, wrecv)
    x_w.start()
    for s in range(dp):
        b += dot(ones, pg_all[s], 1, 1)
    bgrad[r] = b
    x_b = over_row(2, lambda p: bgrad.at[r], bgrad)
    x_b.start()
    x_lgb.wait_recv()
    e = dot(snap_all[0], lg_all[0], 0, 0)
    for s in range(1, dp):
        e += dot(snap_all[s], lg_all[s], 0, 0)
    enc_grad[...] = e
    x_w.forward()
    x_mis.wait_recv()
    x_b.wait_recv()
    x_w.wait_recv()
    for x in (x_adj, x_mis, x_lg, x_pg, x_lgb, x_w, x_b):
        x.wait_send()


def on_device(
    row, dp, snapshots, enc_weight, hidden_weight, hidden_bias, block_weight, block_ids, block_counts
):
    batch = snapshots.shape[0]
    own, slots, blk = block_weight.shape[:3]
    latent = enc_weight.shape[2]
    shard = hidden_weight.shape[0]
    part = shard // row
    tiles = own * dp
    cols = own * blk
    vmem = pl.BlockSpec(memory_space=pltpu.VMEM)
    smem = pl.BlockSpec(memory_space=pltpu.SMEM)
    dma = pltpu.SemaphoreType.DMA
    sds = jax.ShapeDtypeStruct
    bias = jnp.pad(hidden_bias.reshape(row, part), ((0, -row % 16), (0, 0)))
    hid, pre, lat_all, block_all, w_all, snap_all, bias_all = pl.pallas_call(
        functools.partial(forward_kernel, row, dp),
        out_shape=(
            sds((dp, row, part, batch), BF16),
            sds((dp, part, batch), F32),
            sds((dp, batch, latent), BF16),
            sds((dp, own, slots, blk, blk), BF16),
            sds((dp, row, part, latent), BF16),
            sds((dp, batch, cols), BF16),
            sds((dp, *bias.shape), BF16),
        ),
        in_specs=[vmem] * 5,
        out_specs=[vmem] * 7,
        scratch_shapes=[
            pltpu.VMEM((dp, cols, latent), BF16),
            pltpu.VMEM((row, batch, latent), F32),
            dma((3, dp)), dma((3, dp)), dma((3, dp + 1)), dma((3, dp)), dma((row,)), dma((row,)),
            dma((dp, 2 * row)), dma((dp, row)), dma((2,)),
        ],
        compiler_params=pltpu.CompilerParams(
            collective_id=0, has_side_effects=True, vmem_limit_bytes=VMEM_LIMIT
        ),
        name="forward",
    )(
        snapshots,
        enc_weight.reshape(cols, latent),
        hidden_weight.reshape(row, part, latent),
        bias,
        block_weight,
    )
    nblocks = dp * shard // blk
    scale = 1.0 / math.sqrt(batch * dp)
    misfit, adj = pl.pallas_call(
        functools.partial(decode_kernel, scale),
        out_shape=(
            sds((tiles, batch, blk), BF16),
            sds((nblocks, blk, batch), BF16),
        ),
        in_specs=[smem, smem, vmem, vmem, vmem],
        out_specs=[vmem] * 2,
        scratch_shapes=[pltpu.VMEM((nblocks, blk, batch), F32)],
        compiler_params=pltpu.CompilerParams(vmem_limit_bytes=VMEM_LIMIT),
        name="decode",
    )(
        block_ids,
        block_counts,
        hid.reshape(nblocks, blk, batch),
        block_all.reshape(tiles, slots, blk, blk),
        snapshots,
    )
    weight_grad, bias_grad, enc_grad, mis_all = pl.pallas_call(
        functools.partial(backward_kernel, row, dp),
        out_shape=(
            sds((row, part, latent), F32),
            sds((row, 8, part), F32),
            sds((cols, latent), F32),
            sds((dp, own, batch, blk), BF16),
        ),
        in_specs=[vmem] * 6,
        out_specs=[vmem] * 4,
        scratch_shapes=[
            pltpu.VMEM((row, dp, part, batch), BF16),
            pltpu.VMEM((dp, part, batch), BF16),
            pltpu.VMEM((dp, part, batch), BF16),
            pltpu.VMEM((row, batch, latent), F32),
            pltpu.VMEM((dp, batch, latent), BF16),
            dma((3, dp)), dma((3, dp)), dma((3, row)), dma((3, row)), dma((2 * row,)), dma((row,)),
        ],
        compiler_params=pltpu.CompilerParams(
            collective_id=1, has_side_effects=True, vmem_limit_bytes=VMEM_LIMIT
        ),
        name="backward",
    )(
        adj.reshape(dp, row, part, batch),
        misfit.reshape(dp, own, batch, blk),
        pre,
        lat_all,
        w_all,
        snap_all,
    )
    first = lax.axis_index("dp") * own
    bias_lines = bias_all[:, :row].reshape(nblocks, 1, blk)
    block_grad = pl.pallas_call(
        block_grad_kernel,
        out_shape=sds((own, slots, blk, blk), F32),
        in_specs=[smem, smem, vmem, vmem, vmem, vmem],
        out_specs=vmem,
        compiler_params=pltpu.CompilerParams(vmem_limit_bytes=VMEM_LIMIT),
        name="block_grad",
    )(
        lax.dynamic_slice_in_dim(block_ids, first, own),
        lax.dynamic_slice_in_dim(block_counts, first, own),
        w_all.reshape(nblocks, blk, latent),
        jnp.pad(bias_lines, ((0, 0), (0, 15), (0, 0))),
        lat_all,
        mis_all,
    )
    return (
        enc_grad.reshape(own, blk, latent),
        weight_grad.reshape(shard, latent),
        bias_grad[:, 0, :].reshape(shard),
        block_grad,
    )


def solution(mesh):
    in_specs = (
        P(("groups", "dp"), "row"),
        P(("row", "dp"), None, None),
        P("dp", None),
        P("dp"),
        P(("row", "dp"), None, None, None),
        P("row", None),
        P("row"),
    )
    out_specs = (
        P(("groups", "row", "dp"), None, None),
        P(("groups", "dp"), None),
        P(("groups", "dp")),
        P(("groups", "row", "dp"), None, None, None),
    )
    return jax.shard_map(
        functools.partial(on_device, mesh.shape["row"], mesh.shape["dp"]),
        mesh=mesh, in_specs=in_specs, out_specs=out_specs, check_vma=False,
    )
```

time: 216 us -> 159 us (0.74)
  Pallas kernels: 206 us -> 148 us
    pallas_call x1, Pallas kernels: 96.3 us -> 53.9 us  [on_device(): pl.pallas_call(functools.partial(backward_kernel, row, dp), out_shape=(sd...]
    pallas_call x1, Pallas kernels: 100 us -> 76.7 us  [on_device(): pl.pallas_call(functools.partial(forward_kernel, row, dp), out_shape=(sds...]
    pallas_call x0 -> x1, Pallas kernels: none -> 9.13 us  [on_device(): pl.pallas_call(block_grad_kernel, out_shape=sds((own, slots, blk, blk), F...]
    unnamed x5 -> x8, local copies, waits for them, and re-layouts: 5.78 us -> 2.03 us
where the time goes in v2:
time: 159 us; the launch traced here: 157 us
  Pallas kernels  148 us (93%)
  local copies, waits for them, and re-layouts  8.16 us (5%)
    pallas_call x1, Pallas kernels, on_device(): pl.pallas_call(functools.partial(forward_kernel, row, dp), out_shape=(sds...  76.7 us
    pallas_call x1, Pallas kernels, on_device(): pl.pallas_call(functools.partial(backward_kernel, row, dp), out_shape=(sd...  53.9 us
    pallas_call x1, Pallas kernels, on_device(): pl.pallas_call(block_grad_kernel, out_shape=sds((own, slots, blk, blk), F...  9.13 us
    pallas_call x1, Pallas kernels, on_device(): pl.pallas_call(functools.partial(decode_kernel, scale), out_shape=(sds((t...  8.61 us

profile of v2, /device:TPU:11, one launch (start us, length us, event | category | flops | bytes accessed | tf_op | source)
XLA Modules:
  0.0 157.1 jit_solution(15997430148760610257)
XLA Ops:
  0.6 0.7 reshape.43
  1.3 0.6 pad.8.bias
  1.9 76.7 %forward.1 = (bf16[4,4,512,128]{3,2,1,0:T(8,128)(2,1)}, f32[4,512,128]{2,1,0:T(8,128)}, bf16[4,128,256]{2,1,0:T(8,128)(2,1)}, bf16[4,2,8,128,128]{4,3,2,1,0:T(8,...) custom-call(bf16[128,1024]{1,0:T(8,128)(2,1)} %snap.3, ...), custom_call_target="tpu_custom_call" | custom-call | tf_op jit(solution)/shard_map/forward/pallas_call | solution.py:380
  78.6 8.6 %decode.1 = (bf16[8,128,128]{2,1,0:T(8,128)(2,1)}, bf16[64,128,128]{2,1,0:T(8,128)(2,1)}) custom-call(s32[8,8]{1,0:T(8,128)} %ids.1, s32[8]{0:T(128)} %counts.1, bf16[64,128,128]{2,1,0:T(8,128)(2,1)} %bitcast.12, bf16[8,8,128,128]{3,2,1,0:T(8,128)(2,1)} %bitcast.13, bf16[128,1024]{1,0:T(8,128)(2,1)} %snap.3), custom_call_target="tpu_custom_call" | custom-call | tf_op jit(solution)/shard_map/decode/pallas_call | solution.py:412
  87.3 0.0 copy-start.2
  87.3 53.9 %backward.1 = (f32[4,512,256]{2,1,0:T(8,128)}, f32[4,8,512]{2,1,0:T(8,128)}, f32[256,256]{1,0:T(8,128)}, bf16[4,2,128,128]{3,2,1,0:T(8,128)(2,1)}) custom-call(bf16[4,4,512,128]{3,2,1,0:T(8,128)(2,1)} %bitcast.14, bf16[4,2,128,128]{3,2,1,0:T(8,128)(2,1)} %bitcast.16, f32[4,512,128]{2,1,0:T(8,128)} %get-tuple-element.21.pre, ...), custom_call_target="tpu_custom_call" | custom-call | tf_op jit(solution)/shard_map/backward/pallas_call | solution.py:430
  141.1 1.3 constant_dynamic-slice_fusion.ids
  142.4 0.0 copy-done.2
  142.4 0.6 dynamic_slice.7.counts
  143.0 0.8 slice.7
  143.8 0.8 pad.9.bias
  144.5 0.0 copy-start.1
  144.5 0.0 copy-start
  144.5 9.1 %block_grad.1 = f32[2,8,128,128]{3,2,1,0:T(8,128)} custom-call(s32[2,8]{1,0:T(2,128)} %constant_dynamic-slice_fusion.ids, s32[2]{0:T(128)} %dynamic_slice.7.counts, bf16[64,128,256]{2,1,0:T(8,128)(2,1)} %bitcast.10, bf16[64,16,128]{2,1,0:T(8,128)(2,1)} %pad.9.bias, bf16[4,128,256]{2,1,0:T(8,128)(2,1)} %get-tuple-element.22.lat_all.lat, ...), custom_call_target="tpu_custom_call" | custom-call | tf_op jit(solution)/shard_map/block_grad/pallas_call | solution.py:462
  153.6 1.4 slice.6
  155.1 0.0 copy-done.1
  155.1 0.7 copy.14
  155.8 0.0 copy-done
  155.8 1.3 copy.15
  (1 shorter events, 0.0 us)
Async XLA Ops:
  87.3 55.1 %copy-start.2 = (s32[8]{0:T(128)S(1)}, s32[8]{0:T(128)}, u32[]{:S(2)}) copy-start(s32[8]{0:T(128)} %counts.1) | copy-start | bytes 100
  144.5 10.6 %copy-start.1 = (f32[256,256]{1,0:T(8,128)S(1)}, f32[256,256]{1,0:T(8,128)}, u32[]{:S(2)}) copy-start(f32[256,256]{1,0:T(8,128)} %get-tuple-element.25) | copy-start | bytes 786436
  144.5 11.3 %copy-start = (f32[4,512,256]{2,1,0:T(8,128)S(1)}, f32[4,512,256]{2,1,0:T(8,128)}, u32[]{:S(2)}) copy-start(f32[4,512,256]{2,1,0:T(8,128)} %get-tuple-element.26) | copy-start | bytes 6291460

commit v3 on v2

--- a/solution.py
+++ b/solution.py
@@ -109,6 +109,35 @@
             self.each(step, lambda c: c.wait_send())
 
 
+class Spread:
+    def __init__(self, ng, part_of, send, recv):
+        self.ng, self.part_of, self.send, self.recv = ng, part_of, send, recv
+        self.me = lax.axis_index("groups")
+        self.peers = [lax.rem(self.me + i, ng) for i in range(1, ng)]
+
+    def copy(self, slot, part, peer):
+        return pltpu.make_async_remote_copy(
+            src_ref=self.part_of(slot, part),
+            dst_ref=self.part_of(slot, part),
+            send_sem=self.send.at[slot * self.ng + peer],
+            recv_sem=self.recv.at[slot * self.ng + part],
+            device_id={"groups": peer},
+            device_id_type=MESH,
+        )
+
+    def start(self, slot):
+        for p in self.peers:
+            self.copy(slot, self.me, p).start()
+
+    def wait_recv(self, slot):
+        for p in self.peers:
+            self.copy(slot, p, p).wait_recv()
+
+    def wait_send(self, slot):
+        for p in self.peers:
+            self.copy(slot, self.me, p).wait_send()
+
+
 class RowRelay:
     def __init__(self, row, dst_of, send, recv):
         self.row, self.dst_of, self.send, self.recv = row, dst_of, send, recv
@@ -149,14 +178,16 @@
 
 
 def forward_kernel(
-    row, dp, snap, enc, weight, bias, block,
+    ng, row, dp, snap, enc, weight, bias, block,
     hid, pre, lat_all, block_all, w_all, snap_all, bias_all,
-    enc_all, lat_part, dsend, drecv, csend, crecv, rsend, rrecv, wsend, wrecv, lsem,
+    enc_all, lat_part, dsend, drecv, csend, crecv, rsend, rrecv, wsend, wrecv, gsend, grecv, lsem,
 ):
     r, d = lax.axis_index("row"), lax.axis_index("dp")
     cols = snap.shape[1] // dp
     batch = snap.shape[0]
-    greet({"row": row, "dp": dp})
+    g = lax.axis_index("groups")
+    others = [lax.rem(d + i, dp) for i in range(1, dp)]
+    greet({"groups": ng, "row": row, "dp": dp})
 
     def over_dp(k, src_of, dst):
         return Exchange("dp", dp, src_of, lambda s: dst.at[s], dsend.at[k], drecv.at[k])
@@ -167,18 +198,49 @@
     def w_slot(s):
         return RowRelay(row, lambda q: w_all.at[s, q], wsend.at[s], wrecv.at[s])
 
+    def rows_of(size, part):
+        return pl.ds(pl.multiple_of(part * (size // ng), size // ng), size // ng)
+
+    def enc_part(s, part):
+        return enc_all.at[s, rows_of(cols, part)]
+
+    def w_part(s, part):
+        return w_all.at[s, r, rows_of(weight.shape[1], part)]
+
+    def block_part(s, part):
+        return block_all.at[s, rows_of(block.shape[0], part)]
+
+    def shards(step, act):
+        for way in (1, -1):
+            s = d - way * step
+
+            @pl.when((s >= 0) & (s < dp))
+            def _():
+                act(s)
+
+    def w_over_row(s):
+        g_w.wait_recv(s)
+        w_slot(s).start()
+
     def w_arrived(step):
         x_w.forward(step)
-        for way in (1, -1):
-            s = d - way * step
-
-            @pl.when((s >= 0) & (s < dp))
-            def _():
-                w_slot(s).start()
-
-    x_enc = Chain("dp", dp, lambda s: enc_all.at[s], csend.at[0], crecv.at[0])
-    x_w = Chain("dp", dp, lambda s: w_all.at[s, r], csend.at[1], crecv.at[1])
-    x_block = Chain("dp", dp, lambda s: block_all.at[s], csend.at[2], crecv.at[2])
+        shards(step, g_w.start)
+        shards(step, w_over_row)
+
+    def enc_arrived(step):
+        x_enc.forward(step)
+        shards(step, g_enc.start)
+
+    def block_arrived(step):
+        x_block.forward(step)
+        shards(step, g_block.start)
+
+    x_enc = Chain("dp", dp, lambda s: enc_part(s, g), csend.at[0], crecv.at[0])
+    x_w = Chain("dp", dp, lambda s: w_part(s, g), csend.at[1], crecv.at[1])
+    x_block = Chain("dp", dp, lambda s: block_part(s, g), csend.at[2], crecv.at[2])
+    g_enc = Spread(ng, enc_part, gsend.at[0], grecv.at[0])
+    g_w = Spread(ng, w_part, gsend.at[1], grecv.at[1])
+    g_block = Spread(ng, block_part, gsend.at[2], grecv.at[2])
     x_bias = over_dp(0, lambda p: bias, bias_all)
     x_snap = over_dp(1, snap_cols, snap_all)
     own_block = pltpu.make_async_copy(block, block_all.at[d], lsem.at[0])
@@ -193,12 +255,14 @@
     bias_all[d] = bias[...]
     x_bias.start()
     for step in range(1, dp - 1):
-        x_enc.forward(step)
+        enc_arrived(step)
         w_arrived(step)
     own_block.wait()
     x_block.start()
     x_snap.start()
-    x_enc.forward(dp - 1)
+    enc_arrived(dp - 1)
+    for s in others:
+        g_enc.wait_recv(s)
     part = jnp.zeros((batch, enc.shape[1]), F32)
     for s in range(dp):
         part += dot(snap[:, s * cols : (s + 1) * cols], enc_all[s])
@@ -215,7 +279,7 @@
     x_latb = over_dp(2, lambda p: lat_all.at[d], lat_all)
     x_latb.start()
     if dp > 2:
-        x_block.forward(1)
+        block_arrived(1)
     x_bias.wait_recv()
     lines = lax.broadcasted_iota(jnp.int32, (bias.shape[0], batch), 0)
 
@@ -228,7 +292,7 @@
     for s in range(dp):
         w_slot(s).forward()
     for step in range(2, dp - 1):
-        x_block.forward(step)
+        block_arrived(step)
 
     def hid_of(s, _):
         w_slot(s).wait_recv()
@@ -238,11 +302,16 @@
 
     lax.fori_loop(0, dp, hid_of, 0)
     own_snap.wait()
-    x_block.arrived(dp - 1)
+    block_arrived(dp - 1)
+    for s in others:
+        g_block.wait_recv(s)
     for x in (x_latb, x_snap):
         x.wait_recv()
     for x in (x_enc, x_bias, x_w, x_block, x_snap, x_lat, x_latb):
         x.wait_send()
+    for s in others:
+        for x in (g_enc, g_w, g_block):
+            x.wait_send(s)
     for s in range(dp):
         w_slot(s).wait_send()
 
@@ -341,7 +410,7 @@
     ones = jnp.ones((bgrad.shape[1], mis.shape[2]), BF16)
     for s in range(dp):
         w += dot(pg_all[s], lat_all[s])
-    wgrad[r] = w
+    wgrad[r] = w.astype(BF16)
     x_w = RowRelay(row, lambda q: wgrad.at[q], wsend, wrecv)
     x_w.start()
     for s in range(dp):
@@ -363,7 +432,7 @@
 
 
 def on_device(
-    row, dp, snapshots, enc_weight, hidden_weight, hidden_bias, block_weight, block_ids, block_counts
+    ng, row, dp, snapshots, enc_weight, hidden_weight, hidden_bias, block_weight, block_ids, block_counts
 ):
     batch = snapshots.shape[0]
     own, slots, blk = block_weight.shape[:3]
@@ -378,7 +447,7 @@
     sds = jax.ShapeDtypeStruct
     bias = jnp.pad(hidden_bias.reshape(row, part), ((0, -row % 16), (0, 0)))
     hid, pre, lat_all, block_all, w_all, snap_all, bias_all = pl.pallas_call(
-        functools.partial(forward_kernel, row, dp),
+        functools.partial(forward_kernel, ng, row, dp),
         out_shape=(
             sds((dp, row, part, batch), BF16),
             sds((dp, part, batch), F32),
@@ -394,7 +463,8 @@
             pltpu.VMEM((dp, cols, latent), BF16),
             pltpu.VMEM((row, batch, latent), F32),
             dma((3, dp)), dma((3, dp)), dma((3, dp + 1)), dma((3, dp)), dma((row,)), dma((row,)),
-            dma((dp, 2 * row)), dma((dp, row)), dma((2,)),
+            dma((dp, 2 * row)), dma((dp, row)),
+            dma((3, dp * ng)), dma((3, dp * ng)), dma((2,)),
         ],
         compiler_params=pltpu.CompilerParams(
             collective_id=0, has_side_effects=True, vmem_limit_bytes=VMEM_LIMIT
@@ -430,7 +500,7 @@
     weight_grad, bias_grad, enc_grad, mis_all = pl.pallas_call(
         functools.partial(backward_kernel, row, dp),
         out_shape=(
-            sds((row, part, latent), F32),
+            sds((row, part, latent), BF16),
             sds((row, 8, part), F32),
             sds((cols, latent), F32),
             sds((dp, own, batch, blk), BF16),
@@ -476,7 +546,7 @@
     )
     return (
         enc_grad.reshape(own, blk, latent),
-        weight_grad.reshape(shard, latent),
+        weight_grad.reshape(shard, latent).astype(F32),
         bias_grad[:, 0, :].reshape(shard),
         block_grad,
     )
@@ -499,6 +569,6 @@
         P(("groups", "row", "dp"), None, None, None),
     )
     return jax.shard_map(
-        functools.partial(on_device, mesh.shape["row"], mesh.shape["dp"]),
+        functools.partial(on_device, mesh.shape["groups"], mesh.shape["row"], mesh.shape["dp"]),
         mesh=mesh, in_specs=in_specs, out_specs=out_specs, check_vma=False,
     )

time: 159 us -> 144 us (0.906); the launches traced: 157 us -> 144 us
  Pallas kernels: 148 us -> 135 us
    pallas_call x1, Pallas kernels: 76.7 us -> 62 us  [on_device(): pl.pallas_call(functools.partial(forward_kernel, ng, row, dp), out_shape=...]
where the time goes in v3:
time: 144 us
  Pallas kernels  135 us (94%)
  local copies, waits for them, and re-layouts  6.84 us (5%)
  other arithmetic  1.55 us (1%)
    pallas_call x1, Pallas kernels, on_device(): pl.pallas_call(functools.partial(forward_kernel, ng, row, dp), out_shape=...  62 us
    pallas_call x1, Pallas kernels, on_device(): pl.pallas_call(functools.partial(backward_kernel, row, dp), out_shape=(sd...  55 us
    pallas_call x1, Pallas kernels, on_device(): pl.pallas_call(block_grad_kernel, out_shape=sds((own, slots, blk, blk), F...  9.06 us
    pallas_call x1, Pallas kernels, on_device(): pl.pallas_call(functools.partial(decode_kernel, scale), out_shape=(sds((t...  8.62 us

profile of v3, /device:TPU:11, one launch (start us, length us, event | category | flops | bytes accessed | tf_op | source)
XLA Modules:
  0.0 143.7 jit_solution(16097355316772980314)
XLA Ops:
  0.6 0.7 reshape.43
  1.3 0.6 pad.8.bias
  1.9 62.0 %forward.1 = (bf16[4,4,512,128]{3,2,1,0:T(8,128)(2,1)}, f32[4,512,128]{2,1,0:T(8,128)}, bf16[4,128,256]{2,1,0:T(8,128)(2,1)}, bf16[4,2,8,128,128]{4,3,2,1,0:T(8,...) custom-call(bf16[128,1024]{1,0:T(8,128)(2,1)} %snap.3, ...), custom_call_target="tpu_custom_call" | custom-call | tf_op jit(solution)/shard_map/forward/pallas_call | solution.py:449
  64.0 8.6 %decode.1 = (bf16[8,128,128]{2,1,0:T(8,128)(2,1)}, bf16[64,128,128]{2,1,0:T(8,128)(2,1)}) custom-call(s32[8,8]{1,0:T(8,128)} %ids.1, s32[8]{0:T(128)} %counts.1, bf16[64,128,128]{2,1,0:T(8,128)(2,1)} %bitcast.13, bf16[8,8,128,128]{3,2,1,0:T(8,128)(2,1)} %bitcast.14, bf16[128,1024]{1,0:T(8,128)(2,1)} %snap.3), custom_call_target="tpu_custom_call" | custom-call | tf_op jit(solution)/shard_map/decode/pallas_call | solution.py:482
  72.6 0.0 copy-start.2
  72.6 55.0 %backward.1 = (bf16[4,512,256]{2,1,0:T(8,128)(2,1)}, f32[4,8,512]{2,1,0:T(8,128)}, f32[256,256]{1,0:T(8,128)}, bf16[4,2,128,128]{3,2,1,0:T(8,128)(2,1)}) custom-call(bf16[4,4,512,128]{3,2,1,0:T(8,128)(2,1)} %bitcast.15, bf16[4,2,128,128]{3,2,1,0:T(8,128)(2,1)} %bitcast.17, f32[4,512,128]{2,1,0:T(8,128)} %get-tuple-element.21.pre, ...), custom_call_target="tpu_custom_call" | custom-call | tf_op jit(solution)/shard_map/backward/pallas_call | solution.py:500
  127.6 1.3 constant_dynamic-slice_fusion.ids
  128.9 0.0 copy-done.2
  128.9 0.6 dynamic_slice.7.counts
  129.4 0.8 slice.7
  130.2 0.8 pad.9.bias
  131.0 0.0 copy-start
  131.0 9.1 %block_grad.1 = f32[2,8,128,128]{3,2,1,0:T(8,128)} custom-call(s32[2,8]{1,0:T(2,128)} %constant_dynamic-slice_fusion.ids, s32[2]{0:T(128)} %dynamic_slice.7.counts, bf16[64,128,256]{2,1,0:T(8,128)(2,1)} %bitcast.12, bf16[64,16,128]{2,1,0:T(8,128)(2,1)} %pad.9.bias, bf16[4,128,256]{2,1,0:T(8,128)(2,1)} %get-tuple-element.22.lat_all.lat, ...), custom_call_target="tpu_custom_call" | custom-call | tf_op jit(solution)/shard_map/block_grad/pallas_call | solution.py:532
  140.0 0.0 copy-start.1
  140.0 0.0 copy-done
  140.0 1.5 %bitcast_convert_fusion = f32[2048,256]{1,0:T(8,128)} fusion(bf16[4,512,256]{2,1,0:T(8,128)(2,1)S(1)} %copy-done), kind=kLoop, calls=%fused_computation | loop fusion | flops 524288 | bytes 3145728 | tf_op jit(solution)/shard_map/convert_element_type | solution.py:549
  141.6 1.4 %slice.6 = f32[4,1,512]{2,1,0:T(1,128)} slice(f32[4,8,512]{2,1,0:T(8,128)} %get-tuple-element.27), slice={[0:4], [0:1], [0:512]} | slice | bytes 16384 | tf_op jit(solution)/shard_map/slice | solution.py:550
  143.0 0.0 copy-done.1
  143.0 0.7 copy.13
  (1 shorter events, 0.0 us)
Async XLA Ops:
  72.6 56.3 %copy-start.2 = (s32[8]{0:T(128)S(1)}, s32[8]{0:T(128)}, u32[]{:S(2)}) copy-start(s32[8]{0:T(128)} %counts.1) | copy-start | bytes 100
  131.0 9.1 %copy-start = (bf16[4,512,256]{2,1,0:T(8,128)(2,1)S(1)}, bf16[4,512,256]{2,1,0:T(8,128)(2,1)}, u32[]{:S(2)}) copy-start(bf16[4,512,256]{2,1,0:T(8,128)(2,1)} %get-tuple-element.26) | copy-start | bytes 3145732
  140.0 3.0 %copy-start.1 = (f32[256,256]{1,0:T(8,128)S(1)}, f32[256,256]{1,0:T(8,128)}, u32[]{:S(2)}) copy-start(f32[256,256]{1,0:T(8,128)} %get-tuple-element.25) | copy-start | bytes 786436

commit v4 on v3

--- a/solution.py
+++ b/solution.py
@@ -254,12 +254,11 @@
     w_slot(d).start()
     bias_all[d] = bias[...]
     x_bias.start()
+    own_block.wait()
+    x_block.start()
     for step in range(1, dp - 1):
         enc_arrived(step)
         w_arrived(step)
-    own_block.wait()
-    x_block.start()
-    x_snap.start()
     enc_arrived(dp - 1)
     for s in others:
         g_enc.wait_recv(s)
@@ -270,6 +269,8 @@
     x_lat = Exchange("row", row, lambda p: lat_part.at[r], lambda s: lat_part.at[s], rsend, rrecv)
     x_lat.start()
     w_arrived(dp - 1)
+    if dp > 2:
+        block_arrived(1)
     x_lat.wait_recv()
     total = lat_part[0]
     for s in range(1, row):
@@ -278,8 +279,11 @@
     lat_all[d] = latent_b
     x_latb = over_dp(2, lambda p: lat_all.at[d], lat_all)
     x_latb.start()
-    if dp > 2:
-        block_arrived(1)
+    for s in range(dp):
+        w_slot(s).forward()
+    for step in range(2, dp - 1):
+        block_arrived(step)
+    x_snap.start()
     x_bias.wait_recv()
     lines = lax.broadcasted_iota(jnp.int32, (bias.shape[0], batch), 0)
 
@@ -289,10 +293,6 @@
 
     for s in range(dp):
         pre[s] = pre_of(s, r)
-    for s in range(dp):
-        w_slot(s).forward()
-    for step in range(2, dp - 1):
-        block_arrived(step)
 
     def hid_of(s, _):
         w_slot(s).wait_recv()

time: 144 us -> 142 us (0.986)
  Pallas kernels: 135 us -> 132 us
    pallas_call x1, Pallas kernels: 62 us -> 57.2 us  [on_device(): pl.pallas_call(functools.partial(forward_kernel, ng, row, dp), out_shape=...]
    pallas_call x1, Pallas kernels: 55 us -> 57.5 us  [on_device(): pl.pallas_call(functools.partial(backward_kernel, row, dp), out_shape=(sd...]
where the time goes in v4:
time: 142 us; the launch traced here: 141 us
  Pallas kernels  132 us (93%)
  local copies, waits for them, and re-layouts  6.84 us (5%)
  other arithmetic  1.55 us (1%)
    pallas_call x1, Pallas kernels, on_device(): pl.pallas_call(functools.partial(backward_kernel, row, dp), out_shape=(sd...  57.5 us
    pallas_call x1, Pallas kernels, on_device(): pl.pallas_call(functools.partial(forward_kernel, ng, row, dp), out_shape=...  57.2 us
    pallas_call x1, Pallas kernels, on_device(): pl.pallas_call(block_grad_kernel, out_shape=sds((own, slots, blk, blk), F...  9.06 us
    pallas_call x1, Pallas kernels, on_device(): pl.pallas_call(functools.partial(decode_kernel, scale), out_shape=(sds((t...  8.61 us

profile of v4, /device:TPU:11, one launch (start us, length us, event | category | flops | bytes accessed | tf_op | source)
XLA Modules:
  0.0 141.4 jit_solution(15649161906781439063)
XLA Ops:
  0.6 0.7 reshape.43
  1.3 0.6 pad.8.bias
  1.9 57.2 %forward.1 = (bf16[4,4,512,128]{3,2,1,0:T(8,128)(2,1)}, f32[4,512,128]{2,1,0:T(8,128)}, bf16[4,128,256]{2,1,0:T(8,128)(2,1)}, bf16[4,2,8,128,128]{4,3,2,1,0:T(8,...) custom-call(bf16[128,1024]{1,0:T(8,128)(2,1)} %snap.3, ...), custom_call_target="tpu_custom_call" | custom-call | tf_op jit(solution)/shard_map/forward/pallas_call | solution.py:449
  59.2 8.6 %decode.1 = (bf16[8,128,128]{2,1,0:T(8,128)(2,1)}, bf16[64,128,128]{2,1,0:T(8,128)(2,1)}) custom-call(s32[8,8]{1,0:T(8,128)} %ids.1, s32[8]{0:T(128)} %counts.1, bf16[64,128,128]{2,1,0:T(8,128)(2,1)} %bitcast.13, bf16[8,8,128,128]{3,2,1,0:T(8,128)(2,1)} %bitcast.14, bf16[128,1024]{1,0:T(8,128)(2,1)} %snap.3), custom_call_target="tpu_custom_call" | custom-call | tf_op jit(solution)/shard_map/decode/pallas_call | solution.py:482
  67.8 0.0 copy-start.2
  67.8 57.5 %backward.1 = (bf16[4,512,256]{2,1,0:T(8,128)(2,1)}, f32[4,8,512]{2,1,0:T(8,128)}, f32[256,256]{1,0:T(8,128)}, bf16[4,2,128,128]{3,2,1,0:T(8,128)(2,1)}) custom-call(bf16[4,4,512,128]{3,2,1,0:T(8,128)(2,1)} %bitcast.15, bf16[4,2,128,128]{3,2,1,0:T(8,128)(2,1)} %bitcast.17, f32[4,512,128]{2,1,0:T(8,128)} %get-tuple-element.21.pre, ...), custom_call_target="tpu_custom_call" | custom-call | tf_op jit(solution)/shard_map/backward/pallas_call | solution.py:500
  125.2 1.3 constant_dynamic-slice_fusion.ids
  126.5 0.0 copy-done.2
  126.5 0.6 dynamic_slice.7.counts
  127.1 0.8 slice.7
  127.9 0.8 pad.9.bias
  128.6 0.0 copy-start
  128.6 9.1 %block_grad.1 = f32[2,8,128,128]{3,2,1,0:T(8,128)} custom-call(s32[2,8]{1,0:T(2,128)} %constant_dynamic-slice_fusion.ids, s32[2]{0:T(128)} %dynamic_slice.7.counts, bf16[64,128,256]{2,1,0:T(8,128)(2,1)} %bitcast.12, bf16[64,16,128]{2,1,0:T(8,128)(2,1)} %pad.9.bias, bf16[4,128,256]{2,1,0:T(8,128)(2,1)} %get-tuple-element.22.lat_all.lat, ...), custom_call_target="tpu_custom_call" | custom-call | tf_op jit(solution)/shard_map/block_grad/pallas_call | solution.py:532
  137.7 0.0 copy-start.1
  137.7 0.0 copy-done
  137.7 1.5 %bitcast_convert_fusion = f32[2048,256]{1,0:T(8,128)} fusion(bf16[4,512,256]{2,1,0:T(8,128)(2,1)S(1)} %copy-done), kind=kLoop, calls=%fused_computation | loop fusion | flops 524288 | bytes 3145728 | tf_op jit(solution)/shard_map/convert_element_type | solution.py:549
  139.2 1.4 %slice.6 = f32[4,1,512]{2,1,0:T(1,128)} slice(f32[4,8,512]{2,1,0:T(8,128)} %get-tuple-element.27), slice={[0:4], [0:1], [0:512]} | slice | bytes 16384 | tf_op jit(solution)/shard_map/slice | solution.py:550
  140.7 0.0 copy-done.1
  140.7 0.7 copy.13
  (1 shorter events, 0.0 us)
Async XLA Ops:
  67.8 58.7 %copy-start.2 = (s32[8]{0:T(128)S(1)}, s32[8]{0:T(128)}, u32[]{:S(2)}) copy-start(s32[8]{0:T(128)} %counts.1) | copy-start | bytes 100
  128.6 9.1 %copy-start = (bf16[4,512,256]{2,1,0:T(8,128)(2,1)S(1)}, bf16[4,512,256]{2,1,0:T(8,128)(2,1)}, u32[]{:S(2)}) copy-start(bf16[4,512,256]{2,1,0:T(8,128)(2,1)} %get-tuple-element.26) | copy-start | bytes 3145732
  137.7 3.0 %copy-start.1 = (f32[256,256]{1,0:T(8,128)S(1)}, f32[256,256]{1,0:T(8,128)}, u32[]{:S(2)}) copy-start(f32[256,256]{1,0:T(8,128)} %get-tuple-element.25) | copy-start | bytes 786436

commit v5 on v4

--- a/solution.py
+++ b/solution.py
@@ -340,13 +340,14 @@
 
 def block_grad_kernel(ids, counts, w, bias, lat, mis, grad):
     own, slots, blk, _ = grad.shape
+    first = lax.axis_index("dp") * own
     dp = mis.shape[0]
     ones = jnp.ones((bias.shape[1], mis.shape[2]), BF16)
 
     def slot(k, _):
         for t in range(own):
-            j = ids[t, k]
-            live = (k < counts[t]).astype(F32)
+            j = ids[first + t, k]
+            live = (k < counts[first + t]).astype(F32)
             shift = dot(bias[j], ones, 0, 0)
             o = jnp.zeros((blk, blk), F32)
             for s in range(dp):
@@ -361,8 +362,8 @@
 def backward_kernel(
     row, dp, adj, mis, pre, lat_all, w_all, snap_all,
     wgrad, bgrad, enc_grad, mis_all,
-    adj_all, pg, pg_all, lg_part, lg_all,
-    dsend, drecv, rsend, rrecv, wsend, wrecv,
+    sib_adj, pair, adj_all, pg, pg_all, lg_part, lg_all,
+    dsend, drecv, rsend, rrecv, wsend, wrecv, asend, arecv, ssem,
 ):
     r, d = lax.axis_index("row"), lax.axis_index("dp")
     greet({"row": row, "dp": dp})
@@ -373,18 +374,45 @@
     def over_row(k, src_of, dst):
         return Exchange("row", row, src_of, lambda s: dst.at[s], rsend.at[k], rrecv.at[k])
 
-    x_adj = over_row(0, lambda p: adj.at[:, p], adj_all)
-    x_adj.start()
+    y, c = lax.div(r, 2), lax.rem(r, 2)
+    chips = row // 2
+    far = [lax.rem(y + i, chips) for i in range(1, chips)]
+    to_sib = pltpu.make_async_remote_copy(
+        src_ref=adj.at[:, :, 1 - c],
+        dst_ref=sib_adj,
+        send_sem=ssem.at[0],
+        recv_sem=ssem.at[1],
+        device_id={"row": r + 1 - 2 * c},
+        device_id_type=MESH,
+    )
+    to_sib.start()
+
+    def to_chip(p, slot):
+        return pltpu.make_async_remote_copy(
+            src_ref=pair.at[p],
+            dst_ref=adj_all.at[slot],
+            send_sem=asend.at[p],
+            recv_sem=arecv.at[slot],
+            device_id={"row": 2 * p + c},
+            device_id_type=MESH,
+        )
+
     x_mis = over_dp(0, lambda p: mis.at[p], mis_all)
     x_mis.start()
-    adj_all[r] = adj[:, r]
     mis_all[d] = mis[d]
-    x_adj.wait_recv()
+    to_sib.wait_recv()
+    for p in far:
+        for s in range(dp):
+            both = adj[s, p, c].astype(F32) + sib_adj[s, p].astype(F32)
+            pair[p, s] = both.astype(BF16)
+        to_chip(p, y).start()
+    for p in far:
+        to_chip(p, p).wait_recv()
     part = jnp.zeros((mis.shape[2], lat_all.shape[2]), F32)
     for s in range(dp):
-        a = adj_all[0, s].astype(F32)
-        for q in range(1, row):
-            a += adj_all[q, s].astype(F32)
+        a = adj[s, y, c].astype(F32) + sib_adj[s, y].astype(F32)
+        for p in far:
+            a += adj_all[p, s].astype(F32)
         v = pre[s]
         sigma = jax.nn.sigmoid(v)
         g = (a * (sigma * (1.0 + v * (1.0 - sigma)))).astype(BF16)
@@ -427,7 +455,10 @@
     x_mis.wait_recv()
     x_b.wait_recv()
     x_w.wait_recv()
-    for x in (x_adj, x_mis, x_lg, x_pg, x_lgb, x_w, x_b):
+    to_sib.wait_send()
+    for p in far:
+        to_chip(p, y).wait_send()
+    for x in (x_mis, x_lg, x_pg, x_lgb, x_w, x_b):
         x.wait_send()
 
 
@@ -508,26 +539,28 @@
         in_specs=[vmem] * 6,
         out_specs=[vmem] * 4,
         scratch_shapes=[
-            pltpu.VMEM((row, dp, part, batch), BF16),
+            pltpu.VMEM((dp, row // 2, part, batch), BF16),
+            pltpu.VMEM((row // 2, dp, part, batch), BF16),
+            pltpu.VMEM((row // 2, dp, part, batch), BF16),
             pltpu.VMEM((dp, part, batch), BF16),
             pltpu.VMEM((dp, part, batch), BF16),
             pltpu.VMEM((row, batch, latent), F32),
             pltpu.VMEM((dp, batch, latent), BF16),
             dma((3, dp)), dma((3, dp)), dma((3, row)), dma((3, row)), dma((2 * row,)), dma((row,)),
+            dma((row // 2,)), dma((row // 2,)), dma((2,)),
         ],
         compiler_params=pltpu.CompilerParams(
             collective_id=1, has_side_effects=True, vmem_limit_bytes=VMEM_LIMIT
         ),
         name="backward",
     )(
-        adj.reshape(dp, row, part, batch),
+        adj.reshape(dp, row // 2, 2, part, batch),
         misfit.reshape(dp, own, batch, blk),
         pre,
         lat_all,
         w_all,
         snap_all,
     )
-    first = lax.axis_index("dp") * own
     bias_lines = bias_all[:, :row].reshape(nblocks, 1, blk)
     block_grad = pl.pallas_call(
         block_grad_kernel,
@@ -537,8 +570,8 @@
         compiler_params=pltpu.CompilerParams(vmem_limit_bytes=VMEM_LIMIT),
         name="block_grad",
     )(
-        lax.dynamic_slice_in_dim(block_ids, first, own),
-        lax.dynamic_slice_in_dim(block_counts, first, own),
+        block_ids,
+        block_counts,
         w_all.reshape(nblocks, blk, latent),
         jnp.pad(bias_lines, ((0, 0), (0, 15), (0, 0))),
         lat_all,

time: 142 us -> 139 us (0.979)
  local copies, waits for them, and re-layouts: 6.84 us -> 5 us
    dynamic_slice x2 -> x0, local copies, waits for them, and re-layouts: 1.84 us -> none  [the longest x1 1.26 us: on_device(): lax.dynamic_slice_in_dim(block_ids, first, own)]
where the time goes in v5:
time: 139 us
  Pallas kernels  132 us (95%)
  local copies, waits for them, and re-layouts  5 us (4%)
  other arithmetic  1.55 us (1%)
    pallas_call x1, Pallas kernels, on_device(): pl.pallas_call(functools.partial(forward_kernel, ng, row, dp), out_shape=...  57.2 us
    pallas_call x1, Pallas kernels, on_device(): pl.pallas_call(functools.partial(backward_kernel, row, dp), out_shape=(sd...  57 us
    pallas_call x1, Pallas kernels, on_device(): pl.pallas_call(block_grad_kernel, out_shape=sds((own, slots, blk, blk), F...  9.09 us
    pallas_call x1, Pallas kernels, on_device(): pl.pallas_call(functools.partial(decode_kernel, scale), out_shape=(sds((t...  8.61 us

profile of v5, /device:TPU:11, one launch (start us, length us, event | category | flops | bytes accessed | tf_op | source)
XLA Modules:
  0.0 139.1 jit_solution(8082660441518404102)
XLA Ops:
  0.6 0.7 reshape.43
  1.3 0.6 pad.8.bias
  1.9 57.2 %forward.1 = (bf16[4,4,512,128]{3,2,1,0:T(8,128)(2,1)}, f32[4,512,128]{2,1,0:T(8,128)}, bf16[4,128,256]{2,1,0:T(8,128)(2,1)}, bf16[4,2,8,128,128]{4,3,2,1,0:T(8,...) custom-call(bf16[128,1024]{1,0:T(8,128)(2,1)} %snap.3, ...), custom_call_target="tpu_custom_call" | custom-call | tf_op jit(solution)/shard_map/forward/pallas_call | solution.py:480
  59.2 8.6 %decode.1 = (bf16[8,128,128]{2,1,0:T(8,128)(2,1)}, bf16[64,128,128]{2,1,0:T(8,128)(2,1)}) custom-call(s32[8,8]{1,0:T(8,128)} %ids.3, s32[8]{0:T(128)} %counts.3, bf16[64,128,128]{2,1,0:T(8,128)(2,1)} %bitcast.13, bf16[8,8,128,128]{3,2,1,0:T(8,128)(2,1)} %bitcast.14, bf16[128,1024]{1,0:T(8,128)(2,1)} %snap.3), custom_call_target="tpu_custom_call" | custom-call | tf_op jit(solution)/shard_map/decode/pallas_call | solution.py:513
  67.8 57.0 %backward.1 = (bf16[4,512,256]{2,1,0:T(8,128)(2,1)}, f32[4,8,512]{2,1,0:T(8,128)}, f32[256,256]{1,0:T(8,128)}, bf16[4,2,128,128]{3,2,1,0:T(8,128)(2,1)}) custom-call(bf16[4,2,2,512,128]{4,3,2,1,0:T(8,128)(2,1)} %bitcast.15, bf16[4,2,128,128]{3,2,1,0:T(8,128)(2,1)} %bitcast.17, f32[4,512,128]{2,1,0:T(8,128)} %get-tuple-element.21.pre, ...), custom_call_target="tpu_custom_call" | custom-call | tf_op jit(solution)/shard_map/backward/pallas_call | solution.py:531
  124.8 1.4 %slice.6 = f32[4,1,512]{2,1,0:T(1,128)} slice(f32[4,8,512]{2,1,0:T(8,128)} %get-tuple-element.27), slice={[0:4], [0:1], [0:512]} | slice | bytes 16384 | tf_op jit(solution)/shard_map/slice | solution.py:583
  126.2 0.8 slice.7
  127.0 0.8 pad.9.bias
  127.7 0.0 copy-start
  127.7 9.1 %block_grad.1 = f32[2,8,128,128]{3,2,1,0:T(8,128)} custom-call(s32[8,8]{1,0:T(8,128)} %ids.3, s32[8]{0:T(128)} %counts.3, bf16[64,128,256]{2,1,0:T(8,128)(2,1)} %bitcast.12, bf16[64,16,128]{2,1,0:T(8,128)(2,1)} %pad.9.bias, bf16[4,128,256]{2,1,0:T(8,128)(2,1)} %get-tuple-element.22.lat_all.lat, bf16[4,2,128,128]{3,2,1,0:T(8,128)(2,1)} %get-tuple-element.29.mis), custom_call_target="tpu_custom_call" | custom-call | tf_op jit(solution)/shard_map/block_grad/pallas_call | solution.py:565
  136.8 0.0 copy-done
  136.8 0.0 copy-start.1
  136.8 1.5 %bitcast_convert_fusion = f32[2048,256]{1,0:T(8,128)} fusion(bf16[4,512,256]{2,1,0:T(8,128)(2,1)S(1)} %copy-done), kind=kLoop, calls=%fused_computation | loop fusion | flops 524288 | bytes 3145728 | tf_op jit(solution)/shard_map/convert_element_type | solution.py:582
  138.4 0.0 copy-done.1
  138.4 0.7 copy.13
  (1 shorter events, 0.0 us)
Async XLA Ops:
  127.7 9.1 %copy-start = (bf16[4,512,256]{2,1,0:T(8,128)(2,1)S(1)}, bf16[4,512,256]{2,1,0:T(8,128)(2,1)}, u32[]{:S(2)}) copy-start(bf16[4,512,256]{2,1,0:T(8,128)(2,1)} %get-tuple-element.26) | copy-start | bytes 3145732
  136.8 1.6 %copy-start.1 = (f32[256,256]{1,0:T(8,128)S(1)}, f32[256,256]{1,0:T(8,128)}, u32[]{:S(2)}) copy-start(f32[256,256]{1,0:T(8,128)} %get-tuple-element.25) | copy-start | bytes 786436
